TPU v7x, 32 devices: a whole 2x2x4 slice. The times are simulated.
32 devices in a mesh: region: 2 (over y), mod: 4 (over z), obs: 4 (over x, core).
Axes of the slice: x: 2, y: 2, z: 4, core: 2. Of those that a mesh axis runs over, the one named last changes fastest.
Arguments:
- model_days: float32 [16384, 128], P(('region', 'mod')), parts along dimension 0, may hold values from -48 to 48
- obs_days: float32 [16384, 128], P(('region', 'obs', 'mod')), parts along dimension 0, may hold values from -48 to 48
Outputs:
- mapped: float32 [16384, 128], P(('region', 'mod', 'obs')), parts along dimension 0
- row_potential: float32 [16384], P(('region', 'mod')), parts along dimension 0
- col_potential: float32 [16384], P(('region', 'obs')), parts along dimension 0
There are 2 independent parts, one for each index of `region`. A program takes and returns all parts, laid end to end along the dimension named above; each array names one. Nothing has to cross between parts.
All inputs are finite; a program needn't handle non-finite values.
Results may differ from a plain program's by a relative error of at most 0.0003.
Values sent between devices are 32-bit elements; how exact they have to be, the bound alone decides.
A program may use at most 64 MiB of HBM per device.

v0:
```python
import math

import jax
import jax.numpy as jnp
from jax import lax
from jax.sharding import PartitionSpec as P

ITERS = 2


entropy_scale = 0.02


def pair_cost(block_rows, block_square, columns):
    column_square = jnp.sum(columns * columns, axis=1)
    cross = lax.dot_general(
        block_rows,
        columns,
        (((1,), (1,)), ((), ())),
        precision=lax.Precision.HIGHEST,
        preferred_element_type=jnp.float32,
    )
    return (block_square[:, None] + column_square[None, :] - 2.0 * cross) / block_rows.shape[1]


def across_obs(peaks, totals):
    highest = lax.pmax(peaks, "obs")
    summed = lax.psum(totals * jnp.exp(peaks - highest), "obs")
    return highest + jnp.log(summed)


def across_mod(peaks, totals):
    highest = lax.pmax(peaks, "mod")
    summed = lax.psum(totals * jnp.exp(peaks - highest), "mod")
    return highest + jnp.log(summed)


def on_device(model_days, obs_days):
    row_square = jnp.sum(model_days * model_days, axis=1)
    row_count = model_days.shape[0]
    col_count = obs_days.shape[0] * lax.axis_size("mod")
    log_obs = math.log(col_count * lax.axis_size("obs"))
    log_model = math.log(row_count * lax.axis_size("mod"))
    gathered = lax.all_gather(obs_days, "mod", axis=0, tiled=True)
    cost_tile = pair_cost(model_days, row_square, gathered)

    def row_stats(col_potential):
        scores = (col_potential[None, :] - cost_tile) / entropy_scale
        peaks = jnp.max(scores, axis=1)
        return (peaks, jnp.sum(jnp.exp(scores - peaks[:, None]), axis=1))

    col_potential = jnp.zeros((col_count,), jnp.float32)
    for iteration in range(ITERS):
        peaks, totals = row_stats(col_potential)
        row_potential = -entropy_scale * (across_obs(peaks, totals) - log_obs)
        col_scores = (row_potential[:, None] - cost_tile) / entropy_scale
        col_peaks = jnp.max(col_scores, axis=0)
        peaks = col_peaks
        totals = jnp.sum(jnp.exp(col_scores - col_peaks[None, :]), axis=0)
        col_potential = -entropy_scale * (across_mod(peaks, totals) - log_model)
    peaks, totals = row_stats(col_potential)
    final_lse = across_obs(peaks, totals)
    row_potential = -entropy_scale * (final_lse - log_obs)
    weights = jnp.exp((col_potential[None, :] - cost_tile) / entropy_scale - final_lse[:, None])
    partial_map = jnp.dot(
        weights, gathered, precision=lax.Precision.HIGHEST, preferred_element_type=jnp.float32
    )
    summed_map = lax.psum(partial_map, "obs")
    share = row_count // lax.axis_size("obs")
    mapped = lax.dynamic_slice_in_dim(summed_map, lax.axis_index("obs") * share, share, 0)
    return (mapped, row_potential, col_potential)


def solution(mesh):
    in_specs = (P(("region", "mod"), None), P(("region", "obs", "mod"), None))
    out_specs = (P(("region", "mod", "obs"), None), P(("region", "mod")), P(("region", "obs")))
    return jax.shard_map(
        on_device, mesh=mesh, in_specs=in_specs, out_specs=out_specs, check_vma=False
    )
```

profile of v0, /device:TPU:0, one launch (start us, length us, event | category | flops | bytes accessed | tf_op | source)
XLA Modules:
  0.0 285.4 jit_solution(2504910936190339218)
XLA Ops:
  9.5 30.7 %all-gather.2.cloned.1.call-done = f32[2048,128]{1,0:T(8,128)} async-done(((f32[512,128]{1,0:T(8,128)}), f32[2048,128]{1,0:T(8,128)}) %all-gather.2.cloned.1.call-update) | async-done | bytes 1048592 | tf_op jit(solution)/shard_map/all_gather | solution.py:44
  41.8 20.6 %fusion.3 = (f32[2048]{0:T(1024)S(1)}, f32[2048,2048]{0,1:T(8,128)}) fusion(f32[2048,128]{1,0:T(8,128)} %param.2, f32[2048,128]{1,0:T(8,128)} %all-gather.2.cloned.1.call-done, f32[2048]{0:T(1024)S(1)} %multiply_reduce_fusion, f32[2048]{0:T(1024)S(1)} %multiply_reduce_fusion.1), kind=kOutput, calls=%fused_computation.14 | convolution fusion | flops 6471809024 | bytes 18898944 | tf_op jit(solution)/shard_map/dot_general | solution.py:16
  62.4 6.5 %pmax.35 = f32[2048]{0:T(1024)S(1)} all-reduce(f32[2048]{0:T(1024)S(1)} %get-tuple-element.5), channel_id=1, replica_groups=mesh['region'=2,'mod'=4,'obs'=4] {'obs'}, use_global_device_ids=true, to_apply=%region_3.0 | all-reduce | flops 2048 | bytes 16384 | tf_op jit(solution)/shard_map/pmax | solution.py:27
  68.9 9.1 %exponential_reduce_fusion.4 = f32[2048]{0:T(1024)S(1)} fusion(f32[2048,2048]{0,1:T(8,128)} %get-tuple-element.6, f32[2048]{0:T(1024)S(1)} %get-tuple-element.5), kind=kLoop, calls=%fused_computation.11 | loop fusion | flops 16775168 | bytes 16793600 | tf_op jit(solution)/shard_map/reduce_sum | solution.py:50
  78.0 6.1 %psum.42 = f32[2048]{0:T(1024)S(1)} all-reduce(f32[2048]{0:T(1024)S(1)} %exponential_multiply_fusion.4), channel_id=1, replica_groups=mesh['region'=2,'mod'=4,'obs'=4] {'obs'}, use_global_device_ids=true, to_apply=%region_5.0 | all-reduce | flops 2048 | bytes 16384 | tf_op jit(solution)/shard_map/psum | solution.py:28
  84.1 7.5 %fusion.4 = f32[2048]{0:T(1024)S(1)} fusion(f32[2048,2048]{0,1:T(8,128)} %get-tuple-element.6, f32[2048]{0:T(1024)S(1)} %add_multiply_fusion.4), kind=kLoop, calls=%fused_computation.15 | loop fusion | flops 12580864 | bytes 16793600 | tf_op jit(solution)/shard_map/reduce_max | solution.py:57
  91.7 8.0 %exponential_reduce_fusion.3 = f32[2048]{0:T(1024)S(1)} fusion(f32[2048,2048]{0,1:T(8,128)} %get-tuple-element.6, f32[2048]{0:T(1024)S(1)} %fusion.4, f32[2048]{0:T(1024)S(1)} %add_multiply_fusion.4), kind=kLoop, calls=%fused_computation.9 | loop fusion | flops 16775168 | bytes 16801792 | tf_op jit(solution)/shard_map/reduce_sum | solution.py:59
  99.6 11.1 %pmax.36 = f32[2048]{0:T(1024)S(1)} all-reduce(f32[2048]{0:T(1024)S(1)} %fusion.4), channel_id=1, replica_groups=mesh['region'=2,'mod'=4,'obs'=4] {'mod'}, use_global_device_ids=true, to_apply=%region_7.0 | all-reduce | flops 2048 | bytes 16384 | tf_op jit(solution)/shard_map/pmax | solution.py:33
  110.7 8.5 %psum.43 = f32[2048]{0:T(1024)S(1)} all-reduce(f32[2048]{0:T(1024)S(1)} %exponential_multiply_fusion.3), channel_id=1, replica_groups=mesh['region'=2,'mod'=4,'obs'=4] {'mod'}, use_global_device_ids=true, to_apply=%region_9.0 | all-reduce | flops 2048 | bytes 16384 | tf_op jit(solution)/shard_map/psum | solution.py:34
  119.2 7.5 %fusion.5 = f32[2048]{0:T(1024)S(1)} fusion(f32[2048,2048]{0,1:T(8,128)} %get-tuple-element.6, f32[2048]{0:T(1024)S(1)} %add_multiply_fusion.3), kind=kLoop, calls=%fused_computation.16 | loop fusion | flops 12580864 | bytes 16793600 | tf_op jit(solution)/shard_map/reduce_max | solution.py:49
  126.7 8.0 %exponential_reduce_fusion.2 = f32[2048]{0:T(1024)S(1)} fusion(f32[2048,2048]{0,1:T(8,128)} %get-tuple-element.6, f32[2048]{0:T(1024)S(1)} %fusion.5, f32[2048]{0:T(1024)S(1)} %add_multiply_fusion.3), kind=kLoop, calls=%fused_computation.7 | loop fusion | flops 16775168 | bytes 16801792 | tf_op jit(solution)/shard_map/reduce_sum | solution.py:50
  134.7 5.9 %pmax.37 = f32[2048]{0:T(1024)S(1)} all-reduce(f32[2048]{0:T(1024)S(1)} %fusion.5), channel_id=1, replica_groups=mesh['region'=2,'mod'=4,'obs'=4] {'obs'}, use_global_device_ids=true, to_apply=%region_11.0 | all-reduce | flops 2048 | bytes 16384 | tf_op jit(solution)/shard_map/pmax | solution.py:27
  140.6 5.9 %psum.44 = f32[2048]{0:T(1024)S(1)} all-reduce(f32[2048]{0:T(1024)S(1)} %exponential_multiply_fusion.2), channel_id=1, replica_groups=mesh['region'=2,'mod'=4,'obs'=4] {'obs'}, use_global_device_ids=true, to_apply=%region_13.0 | all-reduce | flops 2048 | bytes 16384 | tf_op jit(solution)/shard_map/psum | solution.py:28
  146.5 7.5 %fusion.6 = f32[2048]{0:T(1024)S(1)} fusion(f32[2048,2048]{0,1:T(8,128)} %get-tuple-element.6, f32[2048]{0:T(1024)S(1)} %add_multiply_fusion.2), kind=kLoop, calls=%fused_computation.17 | loop fusion | flops 12580864 | bytes 16793600 | tf_op jit(solution)/shard_map/reduce_max | solution.py:57
  154.0 8.0 %exponential_reduce_fusion.1 = f32[2048]{0:T(1024)S(1)} fusion(f32[2048,2048]{0,1:T(8,128)} %get-tuple-element.6, f32[2048]{0:T(1024)S(1)} %fusion.6, f32[2048]{0:T(1024)S(1)} %add_multiply_fusion.2), kind=kLoop, calls=%fused_computation.5 | loop fusion | flops 16775168 | bytes 16801792 | tf_op jit(solution)/shard_map/reduce_sum | solution.py:59
  162.0 10.6 %pmax.38 = f32[2048]{0:T(1024)S(1)} all-reduce(f32[2048]{0:T(1024)S(1)} %fusion.6), channel_id=1, replica_groups=mesh['region'=2,'mod'=4,'obs'=4] {'mod'}, use_global_device_ids=true, to_apply=%region_15.0 | all-reduce | flops 2048 | bytes 16384 | tf_op jit(solution)/shard_map/pmax | solution.py:33
  172.6 8.7 %psum.45 = f32[2048]{0:T(1024)S(1)} all-reduce(f32[2048]{0:T(1024)S(1)} %exponential_multiply_fusion.1), channel_id=1, replica_groups=mesh['region'=2,'mod'=4,'obs'=4] {'mod'}, use_global_device_ids=true, to_apply=%region_17.0 | all-reduce | flops 2048 | bytes 16384 | tf_op jit(solution)/shard_map/psum | solution.py:34
  181.4 7.6 %fusion.7 = f32[2048]{0:T(1024)S(1)} fusion(f32[2048,2048]{0,1:T(8,128)} %get-tuple-element.6, f32[2048]{0:T(1024)S(1)} %add_multiply_fusion.1), kind=kLoop, calls=%fused_computation.18 | loop fusion | flops 12580864 | bytes 16793600 | tf_op jit(solution)/shard_map/reduce_max | solution.py:49
  189.0 8.0 %exponential_reduce_fusion = f32[2048]{0:T(1024)S(1)} fusion(f32[2048,2048]{0,1:T(8,128)} %get-tuple-element.6, f32[2048]{0:T(1024)S(1)} %fusion.7, f32[2048]{0:T(1024)S(1)} %add_multiply_fusion.1), kind=kLoop, calls=%fused_computation.3 | loop fusion | flops 16775168 | bytes 16801792 | tf_op jit(solution)/shard_map/reduce_sum | solution.py:50
  196.9 5.8 %pmax.39 = f32[2048]{0:T(1024)S(1)} all-reduce(f32[2048]{0:T(1024)S(1)} %fusion.7), channel_id=1, replica_groups=mesh['region'=2,'mod'=4,'obs'=4] {'obs'}, use_global_device_ids=true, to_apply=%region_19.0 | all-reduce | flops 2048 | bytes 16384 | tf_op jit(solution)/shard_map/pmax | solution.py:27
  202.7 6.8 %psum.46 = f32[2048]{0:T(1024)S(1)} all-reduce(f32[2048]{0:T(1024)S(1)} %exponential_multiply_fusion), channel_id=1, replica_groups=mesh['region'=2,'mod'=4,'obs'=4] {'obs'}, use_global_device_ids=true, to_apply=%region_21.0 | all-reduce | flops 2048 | bytes 16384 | tf_op jit(solution)/shard_map/psum | solution.py:28
  210.1 31.6 %fusion = f32[2048,128]{1,0:T(8,128)} fusion(f32[2048,128]{1,0:T(8,128)S(1)} %copy-done, f32[2048,2048]{0,1:T(8,128)} %get-tuple-element.6, f32[2048]{0:T(1024)S(1)} %get-tuple-element.4, f32[2048]{0:T(1024)S(1)} %add_multiply_fusion.1), kind=kOutput, calls=%fused_computation | convolution fusion | flops 6455033856 | bytes 18890752 | tf_op jit(solution)/shard_map/dot_general | solution.py:65
  241.7 35.2 %all-reduce.2.cloned.1.call-done = f32[2048,128]{1,0:T(8,128)} async-done(((f32[2048,128]{1,0:T(8,128)}), f32[2048,128]{1,0:T(8,128)}) %all-reduce.2.cloned.1.call-update) | async-done | bytes 1048592 | tf_op jit(solution)/shard_map/psum | solution.py:68
  276.9 1.7 constant_dynamic-slice_fusion
  (20 shorter events, 4.6 us)
Async XLA Ops:
  7.2 33.1 %all-gather.2.cloned.1.call-start = ((), (), s32[]{:S(2)}) async-start(), calls=%async_computation | async-start | bytes 1310720 | tf_op jit(solution)/shard_map/all_gather | solution.py:44
  7.9 269.0 %all-reduce.2.cloned.1.call-start = ((), (), s32[]{:S(2)}) async-start(), calls=%async_computation.1 | async-start | bytes 2097152 | tf_op jit(solution)/shard_map/psum | solution.py:68
  181.4 28.7 %copy-start.1 = (f32[2048]{0:T(1024)}, f32[2048]{0:T(1024)S(1)}, u32[]{:S(2)}) copy-start(f32[2048]{0:T(1024)S(1)} %add_multiply_fusion.1) | copy-start | bytes 24580
  181.4 28.7 %copy-start = (f32[2048,128]{1,0:T(8,128)S(1)}, f32[2048,128]{1,0:T(8,128)}, u32[]{:S(2)}) copy-start(f32[2048,128]{1,0:T(8,128)} %all-gather.2.cloned.1.call-done) | copy-start | bytes 3145732
Sparse Core Ops, SparseCore 0:
  9.6 30.6 all-gather.1
  241.8 34.9 all-reduce.1
where the time goes:
time: 286 us; the launch traced here: 285 us
  blocking collectives  75.8 us (27%)
  other arithmetic  74.9 us (26%)
  waiting for transfers between devices  66.6 us (23%)
  matrix products  52.2 us (18%)
  between operations  14.2 us (5%)
    psum x1, waiting for transfers between devices, on_device(): summed_map = lax.psum(partial_map, 'obs')  35.2 us
    dot_general x1, matrix products, on_device(): jnp.dot(weights, gathered, precision=lax.Precision.HIGHEST, preferred_ele...  31.6 us
    all_gather x1, waiting for transfers between devices, on_device(): gathered = lax.all_gather(obs_days, 'mod', axis=0, tiled=True)  30.7 us
    reduce_sum x3, other arithmetic, row_stats(): return (peaks, jnp.sum(jnp.exp(scores - peaks[:, None]), axis=1))  25 us
    pmax x2, blocking collectives, across_mod(): highest = lax.pmax(peaks, 'mod')  21.7 us
    dot_general x1, matrix products, pair_cost(): lax.dot_general(block_rows, columns, (((1,), (1,)), ((), ())), precision=...  20.6 us
    psum x3, blocking collectives, across_obs(): summed = lax.psum(totals * jnp.exp(peaks - highest), 'obs')  18.7 us
    pmax x3, blocking collectives, across_obs(): highest = lax.pmax(peaks, 'obs')  18.1 us
  transfers between devices with their start and end apart: 2, of which 2 were waited for; matrix products, arithmetic and copies ran while one was open for 1% of the time, Pallas kernels for 0%

commit v1 on v0

v1 whole, which is shorter than its diff:
```python
import functools
import math

import jax
import jax.numpy as jnp
from jax import lax
from jax.experimental import pallas as pl
from jax.experimental.pallas import tpu as pltpu
from jax.sharding import PartitionSpec as P

ITERS = 2
EPS = 0.02
LOG2E = math.log2(math.e)
LN2 = math.log(2.0)
LANE = 128
F32 = jnp.float32
BF16 = jnp.bfloat16


def split3(x):
    a = x.astype(BF16)
    r = x - a.astype(F32)
    b = r.astype(BF16)
    c = (r - b.astype(F32)).astype(BF16)
    return a, b, c


def log2(x):
    return jnp.log(x) * LOG2E


def to_col(row):
    return jnp.broadcast_to(row, (LANE, LANE)).T


def kernel(n_mod, n_obs, model_ref, obs_ref, map_ref, rowp_ref, colp_ref,
           gath, a_ref, b_ref, c_ref, s_ref, q0_ref, q1_ref, w_ref, peak_col,
           tot_col, l_col, rsq, l1_ref, m_ref, v_ref, xrow, xcol, part, mapx,
           g_send, g_recv, r_send, r_recv, c_send, c_recv, p_send, p_recv):
    rows, feat = model_ref.shape
    depth = obs_ref.shape[0]
    cols = depth * n_mod
    nrb, nct, dt = rows // LANE, cols // LANE, depth // LANE
    scale = LOG2E / EPS
    log_obs = math.log2(cols * n_obs)
    log_mod = math.log2(rows * n_mod)
    me_m, me_o = lax.axis_index("mod"), lax.axis_index("obs")
    mod_peer = lambda k: {"mod": lax.rem(me_m + k, n_mod)}
    obs_peer = lambda k: {"obs": lax.rem(me_o + k, n_obs)}

    barrier = pltpu.get_barrier_semaphore()
    for k in range(1, n_mod):
        pl.semaphore_signal(barrier, inc=1, device_id=mod_peer(k), device_id_type=pl.DeviceIdType.MESH)
    for k in range(1, n_obs):
        pl.semaphore_signal(barrier, inc=1, device_id=obs_peer(k), device_id_type=pl.DeviceIdType.MESH)
    pl.semaphore_wait(barrier, n_mod + n_obs - 2)

    def remote(src, dst, send, recv, peer):
        return pltpu.make_async_remote_copy(
            src_ref=src, dst_ref=dst, send_sem=send, recv_sem=recv,
            device_id=peer, device_id_type=pl.DeviceIdType.MESH)

    near = [k // 2 + 1 if k % 2 == 0 else n_mod - (k + 1) // 2 for k in range(n_mod - 1)]
    gathers = {}
    for k in near:
        gathers[k] = remote(obs_ref, gath.at[me_m], g_send.at[k], g_recv.at[k], mod_peer(k))
        gathers[k].start()

    @pl.loop(0, nrb)
    def _(b):
        blk = model_ref[pl.ds(pl.multiple_of(b * LANE, LANE), LANE), :]
        sq = blk * blk
        rsq[pl.ds(b, 1), :] = jnp.sum(sq.T, axis=0, keepdims=True) * (scale / feat)
        p0, p1, p2 = split3(blk * (2.0 * scale / feat))
        at = pl.ds(pl.multiple_of(b * LANE, LANE), LANE)
        for t, piece in enumerate((p0, p0, p1, p1, p0, p2)):
            a_ref[at, t * feat:(t + 1) * feat] = piece

    gath[me_m] = obs_ref[...]

    mrows = math.gcd(rows, 512)
    for step, k in enumerate([0] + near):
        if k:
            gathers[k].wait_recv()
        owner = lax.rem(me_m + n_mod - k, n_mod)
        for t in range(dt):
            bt = gath[owner, t * LANE:(t + 1) * LANE, :].T
            lanes = slice(t * LANE, (t + 1) * LANE)
            c_ref[:, lanes] = jnp.sum(bt * bt, axis=0, keepdims=True) * (scale / feat)
            p0, p1, p2 = split3(bt)
            for u, piece in enumerate((p0, p1, p0, p1, p2, p0)):
                b_ref[u * feat:(u + 1) * feat, lanes] = piece

        @pl.loop(0, rows // mrows)
        def _(b, owner=owner, step=step):
            at = pl.ds(pl.multiple_of(b * mrows, mrows), mrows)
            x = jnp.dot(a_ref[at, :], b_ref[...], preferred_element_type=F32) - c_ref[...]
            for t in range(dt):
                s_ref[owner * dt + t, at, :] = x[:, t * LANE:(t + 1) * LANE]

        chunk = 64

        @pl.loop(0, rows // chunk)
        def _(b, owner=owner, step=step):
            at = pl.ds(pl.multiple_of(b * chunk, chunk), chunk)
            tiles = [s_ref[owner * dt + t, at, :] for t in range(dt)]
            top = functools.reduce(jnp.maximum, tiles)
            top = jnp.broadcast_to(jnp.max(top, axis=1, keepdims=True), (chunk, LANE))
            if step:
                old = peak_col[at, :]
                top = jnp.maximum(top, old)
            total = functools.reduce(jnp.add, [jnp.exp2(t - top) for t in tiles])
            if step:
                total = total + tot_col[at, :] * jnp.exp2(old - top)
            peak_col[at, :] = top
            tot_col[at, :] = total

    def start_rows(e):
        copies = []
        for k in range(1, n_obs):
            copies.append(remote(xrow.at[e, me_o], xrow.at[e, me_o], r_send.at[e, k], r_recv.at[e, k], obs_peer(k)))
            copies[-1].start()
        return copies

    def start_cols(e):
        copies = []
        for k in range(1, n_mod):
            copies.append(remote(xcol.at[e, me_m], xcol.at[e, me_m], c_send.at[e, k], c_recv.at[e, k], mod_peer(k)))
            copies[-1].start()
        return copies

    def finish(copies):
        for copy in copies:
            copy.wait_recv()
        for copy in copies:
            copy.wait_send()

    def lse_over(buf, e, n):
        values = [buf[e, d] for d in range(n)]
        top = functools.reduce(jnp.maximum, values)
        return top + log2(functools.reduce(jnp.add, [jnp.exp2(v - top) for v in values]))

    def sum_over(buf, e, n):
        return functools.reduce(jnp.add, [buf[e, d] for d in range(n)])

    def spread(value_ref):
        @pl.loop(0, nrb)
        def _(b):
            l_col[pl.ds(pl.multiple_of(b * LANE, LANE), LANE), :] = to_col(value_ref[pl.ds(b, 1), :])

    @pl.loop(0, nrb)
    def _(b):
        at = pl.ds(pl.multiple_of(b * LANE, LANE), LANE)
        total = jnp.sum(tot_col[at, :].T, axis=0, keepdims=True)
        xrow[0, me_o, pl.ds(b, 1), :] = peak_col[at, :].T[0:1, :] + log2(total)

    finish(start_rows(0))
    l1_ref[...] = lse_over(xrow, 0, n_obs)
    spread(l1_ref)

    group = 4
    chunk = 64

    def fold(x, op):
        return op(x.reshape(chunk // 8, 8, LANE), axis=0)

    @pl.loop(0, nct // group)
    def _(g):
        def peaks(b, acc):
            at = pl.ds(pl.multiple_of(b * chunk, chunk), chunk)
            l = l_col[at, :]
            return tuple(jnp.maximum(acc[t], fold(s_ref[g * group + t, at, :] - l, jnp.max)) for t in range(group))

        acc = lax.fori_loop(0, rows // chunk, peaks, (jnp.full((8, LANE), -jnp.inf, F32),) * group)
        top = [jnp.max(a, axis=0, keepdims=True) for a in acc]

        def sums(b, acc):
            at = pl.ds(pl.multiple_of(b * chunk, chunk), chunk)
            l = l_col[at, :]
            out = []
            for t in range(group):
                q = jnp.exp2(s_ref[g * group + t, at, :] - l - top[t])
                s_ref[g * group + t, at, :] = q
                out.append(acc[t] + fold(q, jnp.sum))
            return tuple(out)

        acc = lax.fori_loop(0, rows // chunk, sums, (jnp.zeros((8, LANE), F32),) * group)
        for t in range(group):
            m_ref[pl.ds(g * group + t, 1), :] = top[t]
            total = jnp.sum(acc[t], axis=0, keepdims=True)
            xcol[0, me_m, pl.ds(g * group + t, 1), :] = top[t] + log2(total)

    finish(start_cols(0))
    g_all = lse_over(xcol, 0, n_mod)
    v_ref[...] = jnp.exp2(m_ref[...] - g_all)

    def row_totals(e):
        @pl.loop(0, nrb)
        def _(b):
            at = pl.ds(pl.multiple_of(b * LANE, LANE), LANE)
            acc = s_ref[0, at, :] * v_ref[0:1, :]
            for t in range(1, nct):
                acc = acc + s_ref[t, at, :] * v_ref[t:t + 1, :]
            xrow[e, me_o, pl.ds(b, 1), :] = jnp.sum(acc.T, axis=0, keepdims=True)

    for it in range(1, ITERS):
        row_totals(it)
        copies = start_rows(it)
        if it == 1:
            @pl.loop(0, rows // chunk)
            def _(b):
                at = pl.ds(pl.multiple_of(b * chunk, chunk), chunk)
                for t in range(nct):
                    q = s_ref[t, at, :]
                    hi = q.astype(BF16)
                    q0_ref[at, t * LANE:(t + 1) * LANE] = hi
                    q1_ref[at, t * LANE:(t + 1) * LANE] = (q - hi.astype(F32)).astype(BF16)
        finish(copies)
        rsum = sum_over(xrow, it, n_obs)
        xrow[it, me_o] = 1.0 / rsum

        @pl.loop(0, nrb)
        def _(b, it=it):
            l_col[pl.ds(pl.multiple_of(b * LANE, LANE), LANE), :] = to_col(xrow[it, me_o, pl.ds(b, 1), :])

        @pl.loop(0, nct // group)
        def _(g, it=it):
            def sums(b, acc):
                at = pl.ds(pl.multiple_of(b * chunk, chunk), chunk)
                u = l_col[at, :]
                return tuple(acc[t] + fold(s_ref[g * group + t, at, :] * u, jnp.sum) for t in range(group))

            acc = lax.fori_loop(0, rows // chunk, sums, (jnp.zeros((8, LANE), F32),) * group)
            for t in range(group):
                ct = pl.ds(g * group + t, 1)
                xcol[it, me_m, ct, :] = jnp.sum(acc[t], axis=0, keepdims=True) * v_ref[ct, :]

        finish(start_cols(it))
        csum = sum_over(xcol, it, n_mod)
        v_ref[...] = v_ref[...] / csum
        g_all = g_all + log2(csum)

    colp_ref[...] = (ITERS * (log_mod - log_obs) - g_all) * (EPS * LN2)
    row_totals(ITERS)
    last = start_rows(ITERS)

    @pl.loop(0, nct)
    def _(t):
        at = pl.ds(pl.multiple_of(t * LANE, LANE), LANE)
        o = gath[t // dt, pl.ds(pl.multiple_of(lax.rem(t, dt) * LANE, LANE), LANE), :]
        w = o * to_col(v_ref[pl.ds(t, 1), :])
        hi = w.astype(BF16)
        w_ref[at, 0:feat] = hi
        w_ref[at, feat:2 * feat] = (w - hi.astype(F32)).astype(BF16)

    share = rows // n_obs

    def project(owner):
        at = pl.ds(pl.multiple_of(owner * share, share), share)
        y = jnp.dot(q0_ref[at, :], w_ref[...], preferred_element_type=F32)
        y = y + jnp.dot(q1_ref[at, :], w_ref[...], preferred_element_type=F32)
        return y[:, :feat] + y[:, feat:]

    sends = []
    for k in range(1, n_obs):
        part[k - 1] = project(lax.rem(me_o + k, n_obs))
        sends.append(remote(part.at[k - 1], mapx.at[k - 1], p_send.at[k], p_recv.at[k], obs_peer(k)))
        sends[-1].start()
    map_ref[...] = project(me_o)

    finish(last)
    rsum = sum_over(xrow, ITERS, n_obs)
    rowp_ref[...] = (log_obs - ITERS * (log_mod - log_obs) - l1_ref[...] - log2(rsum) + rsq[...]) * (EPS * LN2)
    l1_ref[...] = 1.0 / rsum
    for k in range(1, n_obs):
        sends[k - 1].wait_recv()
    for b in range(share // LANE):
        at = slice(b * LANE, (b + 1) * LANE)
        y = map_ref[at, :]
        for k in range(1, n_obs):
            y = y + mapx[k - 1, at, :]
        map_ref[at, :] = y * to_col(l1_ref[pl.ds(me_o * (share // LANE) + b, 1), :])
    for k in range(1, n_obs):
        sends[k - 1].wait_send()
    for k in near:
        gathers[k].wait_send()


def on_device(n_mod, n_obs, model_days, obs_days):
    rows, feat = model_days.shape
    depth = obs_days.shape[0]
    cols = depth * n_mod
    share = rows // n_obs
    nrb, nct = rows // LANE, cols // LANE
    vmem = pl.BlockSpec(memory_space=pltpu.VMEM)
    dma = pltpu.SemaphoreType.DMA
    mapped, rowp, colp = pl.pallas_call(
        functools.partial(kernel, n_mod, n_obs),
        out_shape=(
            jax.ShapeDtypeStruct((share, feat), F32),
            jax.ShapeDtypeStruct((nrb, LANE), F32),
            jax.ShapeDtypeStruct((nct, LANE), F32),
        ),
        in_specs=[vmem, vmem],
        out_specs=(vmem, vmem, vmem),
        scratch_shapes=[
            pltpu.VMEM((n_mod, depth, feat), F32),
            pltpu.VMEM((rows, 6 * feat), BF16),
            pltpu.VMEM((6 * feat, depth), BF16),
            pltpu.VMEM((1, depth), F32),
            pltpu.VMEM((nct, rows, LANE), F32),
            pltpu.VMEM((rows, cols), BF16),
            pltpu.VMEM((rows, cols), BF16),
            pltpu.VMEM((cols, 2 * feat), BF16),
            pltpu.VMEM((rows, LANE), F32),
            pltpu.VMEM((rows, LANE), F32),
            pltpu.VMEM((rows, LANE), F32),
            pltpu.VMEM((nrb, LANE), F32),
            pltpu.VMEM((nrb, LANE), F32),
            pltpu.VMEM((nct, LANE), F32),
            pltpu.VMEM((nct, LANE), F32),
            pltpu.VMEM((ITERS + 1, n_obs, nrb, LANE), F32),
            pltpu.VMEM((ITERS, n_mod, nct, LANE), F32),
            pltpu.VMEM((n_obs - 1, share, feat), F32),
            pltpu.VMEM((n_obs - 1, share, feat), F32),
            dma((n_mod,)), dma((n_mod,)),
            dma((ITERS + 1, n_obs)), dma((ITERS + 1, n_obs)),
            dma((ITERS, n_mod)), dma((ITERS, n_mod)),
            dma((n_obs,)), dma((n_obs,)),
        ],
        compiler_params=pltpu.CompilerParams(
            collective_id=0, has_side_effects=True, vmem_limit_bytes=56 * 1024 * 1024),
        cost_estimate=pl.CostEstimate(
            flops=20 * rows * cols * feat, bytes_accessed=8 * rows * feat, transcendentals=3 * rows * cols),
    )(model_days, obs_days)
    return mapped, rowp.reshape(rows), colp.reshape(cols)


def solution(mesh):
    n_mod, n_obs = mesh.shape["mod"], mesh.shape["obs"]
    in_specs = (P(("region", "mod"), None), P(("region", "obs", "mod"), None))
    out_specs = (P(("region", "mod", "obs"), None), P(("region", "mod")), P(("region", "obs")))
    return jax.shard_map(
        functools.partial(on_device, n_mod, n_obs), mesh=mesh,
        in_specs=in_specs, out_specs=out_specs, check_vma=False,
    )
```

time: 286 us -> 94.9 us (0.33)
  Pallas kernels: 0 us -> 89.9 us
  blocking collectives: 75.8 us -> 0 us
  other arithmetic: 74.9 us -> 0 us
  waiting for transfers between devices: 66.6 us -> 0 us
  matrix products: 52.2 us -> 0 us
  between operations: 14.2 us -> 0.65 us
    pallas_call x0 -> x1, Pallas kernels: none -> 89.9 us  [on_device(): pl.pallas_call(functools.partial(kernel, n_mod, n_obs), out_shape=(jax.Sh...]
    dot_general x2 -> x0, matrix products: 52.2 us -> none  [the longest x1 31.6 us: on_device(): jnp.dot(weights, gathered, precision=lax.Precision.HIGHEST, preferred_ele...]
    reduce_sum x7 -> x0, other arithmetic: 44.1 us -> none  [the longest x3 25 us: row_stats(): return (peaks, jnp.sum(jnp.exp(scores - peaks[:, None]), axis=1))]
    pmax x5 -> x0, blocking collectives: 39.8 us -> none  [the longest x2 21.7 us: across_mod(): highest = lax.pmax(peaks, 'mod')]
    psum x5 -> x0, blocking collectives: 36 us -> none  [the longest x3 18.7 us: across_obs(): summed = lax.psum(totals * jnp.exp(peaks - highest), 'obs')]
    psum x1 -> x0, waiting for transfers between devices: 35.2 us -> none  [on_device(): summed_map = lax.psum(partial_map, 'obs')]
    all_gather x1 -> x0, waiting for transfers between devices: 30.7 us -> none  [on_device(): gathered = lax.all_gather(obs_days, 'mod', axis=0, tiled=True)]
    reduce_max x4 -> x0, other arithmetic: 30.1 us -> none  [the longest x2 15.1 us: on_device(): col_peaks = jnp.max(col_scores, axis=0)]
  transfers between devices with their start and end apart: 2 -> 0, of which waited for: 2 -> 0; matrix products, arithmetic and copies ran while one was open for 1% -> 0% of each run, Pallas kernels for 0% -> 0%
where the time goes in v1:
time: 94.9 us; the launch traced here: 93.5 us
  Pallas kernels  89.9 us (95%)
  local copies, waits for them, and re-layouts  2.98 us (3%)
    pallas_call x1, Pallas kernels, on_device(): pl.pallas_call(functools.partial(kernel, n_mod, n_obs), out_shape=(jax.Sh...  89.9 us
    unnamed x7, local copies, waits for them, and re-layouts  2.98 us

profile of v1, /device:TPU:0, one launch (start us, length us, event | category | flops | bytes accessed | tf_op | source)
XLA Modules:
  0.0 93.5 jit_solution(3930919037683540702)
XLA Ops:
  0.6 89.9 %shard_map.49 = (f32[512,128]{1,0:T(8,128)}, f32[16,128]{1,0:T(8,128)}, f32[16,128]{1,0:T(8,128)}) custom-call(f32[2048,128]{1,0:T(8,128)} %model_ref.1, f32[512,128]{1,0:T(8,128)} %obs_ref.1), custom_call_target="tpu_custom_call" | custom-call | flops 10737418240 | bytes 2097152 | tf_op jit(solution)/shard_map/pallas_call | solution.py:297
  90.5 0.0 copy-start.1
  90.5 1.7 %copy.8 = f32[512,128]{1,0:T(8,128)} copy(f32[512,128]{1,0:T(8,128)} %get-tuple-element.12) | data formatting | bytes 524288
  92.2 0.0 copy-done.1
  92.2 0.0 copy-start
  92.2 0.6 copy.9
  92.8 0.1 copy-done
  92.9 0.6 copy.10
Async XLA Ops:
  90.5 1.7 %copy-start.1 = (f32[16,128]{1,0:T(8,128)S(1)}, f32[16,128]{1,0:T(8,128)}, u32[]{:S(2)}) copy-start(f32[16,128]{1,0:T(8,128)} %get-tuple-element.7) | copy-start | bytes 24580
  92.2 0.7 copy-start

commit v2 on v1

--- a/solution.py
+++ b/solution.py
@@ -35,7 +35,7 @@
 
 def kernel(n_mod, n_obs, model_ref, obs_ref, map_ref, rowp_ref, colp_ref,
            gath, a_ref, b_ref, c_ref, s_ref, q0_ref, q1_ref, w_ref, peak_col,
-           tot_col, l_col, rsq, l1_ref, m_ref, v_ref, xrow, xcol, part, mapx,
+           tot_col, l_col, rsq, l1_ref, m_ref, v_ref, xrow, xcol, part, half, keep, mapx,
            g_send, g_recv, r_send, r_recv, c_send, c_recv, p_send, p_recv):
     rows, feat = model_ref.shape
     depth = obs_ref.shape[0]
@@ -53,18 +53,10 @@
         pl.semaphore_signal(barrier, inc=1, device_id=mod_peer(k), device_id_type=pl.DeviceIdType.MESH)
     for k in range(1, n_obs):
         pl.semaphore_signal(barrier, inc=1, device_id=obs_peer(k), device_id_type=pl.DeviceIdType.MESH)
-    pl.semaphore_wait(barrier, n_mod + n_obs - 2)
-
     def remote(src, dst, send, recv, peer):
         return pltpu.make_async_remote_copy(
             src_ref=src, dst_ref=dst, send_sem=send, recv_sem=recv,
             device_id=peer, device_id_type=pl.DeviceIdType.MESH)
-
-    near = [k // 2 + 1 if k % 2 == 0 else n_mod - (k + 1) // 2 for k in range(n_mod - 1)]
-    gathers = {}
-    for k in near:
-        gathers[k] = remote(obs_ref, gath.at[me_m], g_send.at[k], g_recv.at[k], mod_peer(k))
-        gathers[k].start()
 
     @pl.loop(0, nrb)
     def _(b):
@@ -76,13 +68,59 @@
         for t, piece in enumerate((p0, p0, p1, p1, p0, p2)):
             a_ref[at, t * feat:(t + 1) * feat] = piece
 
+    pl.semaphore_wait(barrier, n_mod + n_obs - 2)
+
+    right, left = {"mod": lax.rem(me_m + 1, n_mod)}, {"mod": lax.rem(me_m + n_mod - 1, n_mod)}
+    has_right, has_left = me_m < n_mod - 1, me_m > 0
+    inside = jnp.logical_and(has_right, has_left)
+    n_left, n_right = me_m, n_mod - 1 - me_m
+    both = jnp.minimum(n_left, n_right)
+
+    def block_at(j):
+        paired = (j - 1) < 2 * both
+        far = jnp.where(paired, (j - 1) // 2 + 1, j - both)
+        to_left = jnp.where(paired, (j - 1) % 2 == 0, n_left > n_right)
+        return jnp.where(to_left, me_m - far, me_m + far)
+
+    def own_to(peer, sem):
+        return remote(obs_ref, gath.at[me_m], g_send.at[sem], g_recv.at[me_m], peer)
+
+    def pass_on(block, peer):
+        return remote(gath.at[block], gath.at[block], g_send.at[block], g_recv.at[block], peer)
+
+    def each_send(block, act):
+        @pl.when(jnp.logical_and(block < me_m, has_right))
+        def _():
+            act(pass_on(block, right))
+
+        @pl.when(jnp.logical_and(block > me_m, has_left))
+        def _():
+            act(pass_on(block, left))
+
+    def own_sends(act):
+        @pl.when(has_right)
+        def _():
+            act(own_to(right, me_m))
+
+        @pl.when(has_left)
+        def _():
+            act(own_to(left, n_mod))
+
+    def arrive(j):
+        block = block_at(j)
+        pass_on(block, right).wait_recv()
+        each_send(block, lambda copy: copy.start())
+
+    own_sends(lambda copy: copy.start())
     gath[me_m] = obs_ref[...]
 
     mrows = math.gcd(rows, 512)
-    for step, k in enumerate([0] + near):
-        if k:
-            gathers[k].wait_recv()
-        owner = lax.rem(me_m + n_mod - k, n_mod)
+    for step in range(n_mod):
+        if step == 1:
+            arrive(1)
+        if step and step + 1 < n_mod:
+            pl.when(inside)(functools.partial(arrive, step + 1))
+        owner = block_at(step) if step else me_m
         for t in range(dt):
             bt = gath[owner, t * LANE:(t + 1) * LANE, :].T
             lanes = slice(t * LANE, (t + 1) * LANE)
@@ -100,12 +138,11 @@
 
         chunk = 64
 
-        @pl.loop(0, rows // chunk)
+        @pl.loop(0, rows // chunk, unroll=2)
         def _(b, owner=owner, step=step):
             at = pl.ds(pl.multiple_of(b * chunk, chunk), chunk)
             tiles = [s_ref[owner * dt + t, at, :] for t in range(dt)]
             top = functools.reduce(jnp.maximum, tiles)
-            top = jnp.broadcast_to(jnp.max(top, axis=1, keepdims=True), (chunk, LANE))
             if step:
                 old = peak_col[at, :]
                 top = jnp.maximum(top, old)
@@ -115,6 +152,9 @@
             peak_col[at, :] = top
             tot_col[at, :] = total
 
+        if step and step + 1 < n_mod:
+            pl.when(jnp.logical_not(inside))(functools.partial(arrive, step + 1))
+
     def start_rows(e):
         copies = []
         for k in range(1, n_obs):
@@ -151,15 +191,17 @@
     @pl.loop(0, nrb)
     def _(b):
         at = pl.ds(pl.multiple_of(b * LANE, LANE), LANE)
-        total = jnp.sum(tot_col[at, :].T, axis=0, keepdims=True)
-        xrow[0, me_o, pl.ds(b, 1), :] = peak_col[at, :].T[0:1, :] + log2(total)
+        peaks = peak_col[at, :].T
+        top = jnp.max(peaks, axis=0, keepdims=True)
+        total = jnp.sum(tot_col[at, :].T * jnp.exp2(peaks - top), axis=0, keepdims=True)
+        xrow[0, me_o, pl.ds(b, 1), :] = top + log2(total)
 
     finish(start_rows(0))
     l1_ref[...] = lse_over(xrow, 0, n_obs)
     spread(l1_ref)
 
     group = 4
-    chunk = 64
+    chunk = 128
 
     def fold(x, op):
         return op(x.reshape(chunk // 8, 8, LANE), axis=0)
@@ -261,29 +303,42 @@
         y = y + jnp.dot(q1_ref[at, :], w_ref[...], preferred_element_type=F32)
         return y[:, :feat] + y[:, feat:]
 
-    sends = []
-    for k in range(1, n_obs):
-        part[k - 1] = project(lax.rem(me_o + k, n_obs))
-        sends.append(remote(part.at[k - 1], mapx.at[k - 1], p_send.at[k], p_recv.at[k], obs_peer(k)))
-        sends[-1].start()
-    map_ref[...] = project(me_o)
+    chips = n_obs // 2
+    chip, core = me_o // 2, lax.rem(me_o, 2)
+    mate = {"obs": chip * 2 + 1 - core}
+    halves, sends = [], []
+    for d in list(range(1, chips)) + [0]:
+        there = lax.rem(chip + d, chips) * 2
+        part[d] = project(there + 1 - core)
+        halves.append(remote(part.at[d], half.at[d], p_send.at[d], p_recv.at[d], mate))
+        halves[-1].start()
+        mine = project(there + core)
+        if d:
+            halves[-1].wait_recv()
+            keep[d - 1] = mine + half[d]
+            sends.append(remote(keep.at[d - 1], mapx.at[d - 1], p_send.at[chips + d], p_recv.at[chips + d], {"obs": there + core}))
+            sends[-1].start()
+        else:
+            map_ref[...] = mine
 
     finish(last)
     rsum = sum_over(xrow, ITERS, n_obs)
     rowp_ref[...] = (log_obs - ITERS * (log_mod - log_obs) - l1_ref[...] - log2(rsum) + rsq[...]) * (EPS * LN2)
     l1_ref[...] = 1.0 / rsum
-    for k in range(1, n_obs):
-        sends[k - 1].wait_recv()
+    halves[-1].wait_recv()
+    for copy in sends:
+        copy.wait_recv()
     for b in range(share // LANE):
         at = slice(b * LANE, (b + 1) * LANE)
-        y = map_ref[at, :]
-        for k in range(1, n_obs):
-            y = y + mapx[k - 1, at, :]
+        y = map_ref[at, :] + half[0, at, :]
+        for d in range(1, chips):
+            y = y + mapx[d - 1, at, :]
         map_ref[at, :] = y * to_col(l1_ref[pl.ds(me_o * (share // LANE) + b, 1), :])
-    for k in range(1, n_obs):
-        sends[k - 1].wait_send()
-    for k in near:
-        gathers[k].wait_send()
+    for copy in halves + sends:
+        copy.wait_send()
+    own_sends(lambda copy: copy.wait_send())
+    for step in range(1, n_mod):
+        each_send(block_at(step), lambda copy: copy.wait_send())
 
 
 def on_device(n_mod, n_obs, model_days, obs_days):
@@ -321,9 +376,11 @@
             pltpu.VMEM((nct, LANE), F32),
             pltpu.VMEM((ITERS + 1, n_obs, nrb, LANE), F32),
             pltpu.VMEM((ITERS, n_mod, nct, LANE), F32),
-            pltpu.VMEM((n_obs - 1, share, feat), F32),
-            pltpu.VMEM((n_obs - 1, share, feat), F32),
-            dma((n_mod,)), dma((n_mod,)),
+            pltpu.VMEM((n_obs // 2, share, feat), F32),
+            pltpu.VMEM((n_obs // 2, share, feat), F32),
+            pltpu.VMEM((n_obs // 2 - 1, share, feat), F32),
+            pltpu.VMEM((n_obs // 2 - 1, share, feat), F32),
+            dma((n_mod + 1,)), dma((n_mod,)),
             dma((ITERS + 1, n_obs)), dma((ITERS + 1, n_obs)),
             dma((ITERS, n_mod)), dma((ITERS, n_mod)),
             dma((n_obs,)), dma((n_obs,)),

time: 94.9 us -> 80.4 us (0.85); the launches traced: 93.5 us -> 80.2 us
  Pallas kernels: 89.9 us -> 76.5 us
    pallas_call x1, Pallas kernels: 89.9 us -> 76.5 us  [on_device(): pl.pallas_call(functools.partial(kernel, n_mod, n_obs), out_shape=(jax.Sh...]
where the time goes in v2:
time: 80.4 us; the launch traced here: 80.2 us
  Pallas kernels  76.5 us (95%)
  local copies, waits for them, and re-layouts  2.98 us (4%)
    pallas_call x1, Pallas kernels, on_device(): pl.pallas_call(functools.partial(kernel, n_mod, n_obs), out_shape=(jax.Sh...  76.5 us
    unnamed x7, local copies, waits for them, and re-layouts  2.98 us

profile of v2, /device:TPU:0, one launch (start us, length us, event | category | flops | bytes accessed | tf_op | source)
XLA Modules:
  0.0 80.2 jit_solution(8071762950636386752)
XLA Ops:
  0.6 76.5 %shard_map.49 = (f32[512,128]{1,0:T(8,128)}, f32[16,128]{1,0:T(8,128)}, f32[16,128]{1,0:T(8,128)}) custom-call(f32[2048,128]{1,0:T(8,128)} %model_ref.1, f32[512,128]{1,0:T(8,128)} %obs_ref.1), custom_call_target="tpu_custom_call" | custom-call | flops 10737418240 | bytes 2097152 | tf_op jit(solution)/shard_map/pallas_call | solution.py:352
  77.2 0.0 copy-start.1
  77.2 1.7 %copy.8 = f32[512,128]{1,0:T(8,128)} copy(f32[512,128]{1,0:T(8,128)} %get-tuple-element.12) | data formatting | bytes 524288
  78.9 0.0 copy-done.1
  78.9 0.0 copy-start
  78.9 0.6 copy.9
  79.5 0.1 copy-done
  79.6 0.6 copy.10
Async XLA Ops:
  77.2 1.7 %copy-start.1 = (f32[16,128]{1,0:T(8,128)S(1)}, f32[16,128]{1,0:T(8,128)}, u32[]{:S(2)}) copy-start(f32[16,128]{1,0:T(8,128)} %get-tuple-element.7) | copy-start | bytes 24580
  78.9 0.7 copy-start

commit v3 on v2

--- a/solution.py
+++ b/solution.py
@@ -297,8 +297,10 @@
 
     share = rows // n_obs
 
-    def project(owner):
-        at = pl.ds(pl.multiple_of(owner * share, share), share)
+    piece = share // 2
+
+    def project(owner, h):
+        at = pl.ds(pl.multiple_of(owner * share + h * piece, piece), piece)
         y = jnp.dot(q0_ref[at, :], w_ref[...], preferred_element_type=F32)
         y = y + jnp.dot(q1_ref[at, :], w_ref[...], preferred_element_type=F32)
         return y[:, :feat] + y[:, feat:]
@@ -309,24 +311,25 @@
     halves, sends = [], []
     for d in list(range(1, chips)) + [0]:
         there = lax.rem(chip + d, chips) * 2
-        part[d] = project(there + 1 - core)
-        halves.append(remote(part.at[d], half.at[d], p_send.at[d], p_recv.at[d], mate))
-        halves[-1].start()
-        mine = project(there + core)
-        if d:
-            halves[-1].wait_recv()
-            keep[d - 1] = mine + half[d]
-            sends.append(remote(keep.at[d - 1], mapx.at[d - 1], p_send.at[chips + d], p_recv.at[chips + d], {"obs": there + core}))
-            sends[-1].start()
-        else:
-            map_ref[...] = mine
+        for h in range(2):
+            at = slice(h * piece, (h + 1) * piece)
+            part[d, at, :] = project(there + 1 - core, h)
+            halves.append(remote(part.at[d, at], half.at[d, at], p_send.at[0, d, h], p_recv.at[0, d, h], mate))
+            halves[-1].start()
+            mine = project(there + core, h)
+            if d:
+                halves[-1].wait_recv()
+                keep[d - 1, at, :] = mine + half[d, at, :]
+                sends.append(remote(keep.at[d - 1, at], mapx.at[d - 1, at], p_send.at[1, d, h], p_recv.at[1, d, h], {"obs": there + core}))
+                sends[-1].start()
+            else:
+                map_ref[at, :] = mine
 
     finish(last)
     rsum = sum_over(xrow, ITERS, n_obs)
     rowp_ref[...] = (log_obs - ITERS * (log_mod - log_obs) - l1_ref[...] - log2(rsum) + rsq[...]) * (EPS * LN2)
     l1_ref[...] = 1.0 / rsum
-    halves[-1].wait_recv()
-    for copy in sends:
+    for copy in halves[-2:] + sends:
         copy.wait_recv()
     for b in range(share // LANE):
         at = slice(b * LANE, (b + 1) * LANE)
@@ -383,7 +386,7 @@
             dma((n_mod + 1,)), dma((n_mod,)),
             dma((ITERS + 1, n_obs)), dma((ITERS + 1, n_obs)),
             dma((ITERS, n_mod)), dma((ITERS, n_mod)),
-            dma((n_obs,)), dma((n_obs,)),
+            dma((2, n_obs // 2, 2)), dma((2, n_obs // 2, 2)),
         ],
         compiler_params=pltpu.CompilerParams(
             collective_id=0, has_side_effects=True, vmem_limit_bytes=56 * 1024 * 1024),

time: 80.4 us -> 79.2 us (0.985)
  Pallas kernels: 76.5 us -> 75.3 us
    pallas_call x1, Pallas kernels: 76.5 us -> 75.3 us  [on_device(): pl.pallas_call(functools.partial(kernel, n_mod, n_obs), out_shape=(jax.Sh...]
where the time goes in v3:
time: 79.2 us; the launch traced here: 79 us
  Pallas kernels  75.3 us (95%)
  local copies, waits for them, and re-layouts  2.98 us (4%)
    pallas_call x1, Pallas kernels, on_device(): pl.pallas_call(functools.partial(kernel, n_mod, n_obs), out_shape=(jax.Sh...  75.3 us
    unnamed x7, local copies, waits for them, and re-layouts  2.98 us

profile of v3, /device:TPU:0, one launch (start us, length us, event | category | flops | bytes accessed | tf_op | source)
XLA Modules:
  0.0 79.0 jit_solution(10031425321030221865)
XLA Ops:
  0.6 75.3 %shard_map.49 = (f32[512,128]{1,0:T(8,128)}, f32[16,128]{1,0:T(8,128)}, f32[16,128]{1,0:T(8,128)}) custom-call(f32[2048,128]{1,0:T(8,128)} %model_ref.1, f32[512,128]{1,0:T(8,128)} %obs_ref.1), custom_call_target="tpu_custom_call" | custom-call | flops 10737418240 | bytes 2097152 | tf_op jit(solution)/shard_map/pallas_call | solution.py:355
  76.0 0.0 copy-start.1
  76.0 1.7 %copy.8 = f32[512,128]{1,0:T(8,128)} copy(f32[512,128]{1,0:T(8,128)} %get-tuple-element.12) | data formatting | bytes 524288
  77.7 0.0 copy-done.1
  77.7 0.0 copy-start
  77.7 0.6 copy.9
  78.3 0.1 copy-done
  78.4 0.6 copy.10
Async XLA Ops:
  76.0 1.7 %copy-start.1 = (f32[16,128]{1,0:T(8,128)S(1)}, f32[16,128]{1,0:T(8,128)}, u32[]{:S(2)}) copy-start(f32[16,128]{1,0:T(8,128)} %get-tuple-element.7) | copy-start | bytes 24580
  77.7 0.7 copy-start

commit v4 on v3

--- a/solution.py
+++ b/solution.py
@@ -34,7 +34,7 @@
 
 
 def kernel(n_mod, n_obs, model_ref, obs_ref, map_ref, rowp_ref, colp_ref,
-           gath, a_ref, b_ref, c_ref, s_ref, q0_ref, q1_ref, w_ref, peak_col,
+           gath, a_ref, b_ref, c_ref, s_ref, q_ref, w_ref, peak_col,
            tot_col, l_col, rsq, l1_ref, m_ref, v_ref, xrow, xcol, part, half, keep, mapx,
            g_send, g_recv, r_send, r_recv, c_send, c_recv, p_send, p_recv):
     rows, feat = model_ref.shape
@@ -202,6 +202,8 @@
 
     group = 4
     chunk = 128
+    share = rows // n_obs
+    piece = share // 2
 
     def fold(x, op):
         return op(x.reshape(chunk // 8, 8, LANE), axis=0)
@@ -252,11 +254,14 @@
             @pl.loop(0, rows // chunk)
             def _(b):
                 at = pl.ds(pl.multiple_of(b * chunk, chunk), chunk)
+                base = lax.div(b, piece // chunk) * (2 * piece) + lax.rem(b, piece // chunk) * chunk
+                top = pl.ds(pl.multiple_of(base, chunk), chunk)
+                low = pl.ds(pl.multiple_of(base + piece, chunk), chunk)
                 for t in range(nct):
                     q = s_ref[t, at, :]
                     hi = q.astype(BF16)
-                    q0_ref[at, t * LANE:(t + 1) * LANE] = hi
-                    q1_ref[at, t * LANE:(t + 1) * LANE] = (q - hi.astype(F32)).astype(BF16)
+                    q_ref[top, t * LANE:(t + 1) * LANE] = hi
+                    q_ref[low, t * LANE:(t + 1) * LANE] = (q - hi.astype(F32)).astype(BF16)
         finish(copies)
         rsum = sum_over(xrow, it, n_obs)
         xrow[it, me_o] = 1.0 / rsum
@@ -295,14 +300,11 @@
         w_ref[at, 0:feat] = hi
         w_ref[at, feat:2 * feat] = (w - hi.astype(F32)).astype(BF16)
 
-    share = rows // n_obs
-
-    piece = share // 2
 
     def project(owner, h):
-        at = pl.ds(pl.multiple_of(owner * share + h * piece, piece), piece)
-        y = jnp.dot(q0_ref[at, :], w_ref[...], preferred_element_type=F32)
-        y = y + jnp.dot(q1_ref[at, :], w_ref[...], preferred_element_type=F32)
+        at = pl.ds(pl.multiple_of((owner * 2 + h) * (2 * piece), 2 * piece), 2 * piece)
+        y = jnp.dot(q_ref[at, :], w_ref[...], preferred_element_type=F32)
+        y = y[:piece] + y[piece:]
         return y[:, :feat] + y[:, feat:]
 
     chips = n_obs // 2
@@ -367,8 +369,7 @@
             pltpu.VMEM((6 * feat, depth), BF16),
             pltpu.VMEM((1, depth), F32),
             pltpu.VMEM((nct, rows, LANE), F32),
-            pltpu.VMEM((rows, cols), BF16),
-            pltpu.VMEM((rows, cols), BF16),
+            pltpu.VMEM((2 * rows, cols), BF16),
             pltpu.VMEM((cols, 2 * feat), BF16),
             pltpu.VMEM((rows, LANE), F32),
             pltpu.VMEM((rows, LANE), F32),

time: 79.2 us -> 78.9 us (level)
  no operation moved by 1% of the time
where the time goes in v4:
time: 78.9 us; the launch traced here: 78.7 us
  Pallas kernels  75.1 us (95%)
  local copies, waits for them, and re-layouts  2.98 us (4%)
    pallas_call x1, Pallas kernels, on_device(): pl.pallas_call(functools.partial(kernel, n_mod, n_obs), out_shape=(jax.Sh...  75.1 us
    unnamed x7, local copies, waits for them, and re-layouts  2.98 us

profile of v4, /device:TPU:0, one launch (start us, length us, event | category | flops | bytes accessed | tf_op | source)
XLA Modules:
  0.0 78.7 jit_solution(16813025443229921152)
XLA Ops:
  0.6 75.1 %shard_map.49 = (f32[512,128]{1,0:T(8,128)}, f32[16,128]{1,0:T(8,128)}, f32[16,128]{1,0:T(8,128)}) custom-call(f32[2048,128]{1,0:T(8,128)} %model_ref.1, f32[512,128]{1,0:T(8,128)} %obs_ref.1), custom_call_target="tpu_custom_call" | custom-call | flops 10737418240 | bytes 2097152 | tf_op jit(solution)/shard_map/pallas_call | solution.py:357
  75.7 0.0 copy-start.1
  75.7 1.7 %copy.8 = f32[512,128]{1,0:T(8,128)} copy(f32[512,128]{1,0:T(8,128)} %get-tuple-element.12) | data formatting | bytes 524288
  77.4 0.0 copy-done.1
  77.4 0.0 copy-start
  77.4 0.6 copy.9
  78.0 0.1 copy-done
  78.1 0.6 copy.10
Async XLA Ops:
  75.7 1.7 %copy-start.1 = (f32[16,128]{1,0:T(8,128)S(1)}, f32[16,128]{1,0:T(8,128)}, u32[]{:S(2)}) copy-start(f32[16,128]{1,0:T(8,128)} %get-tuple-element.7) | copy-start | bytes 24580
  77.4 0.7 copy-start
